TPU v7x, 32 devices: a whole 2x2x4 slice. The times are simulated.
32 devices in a mesh: dp: 8 (over z, x), fsdp: 4 (over y, core).
Axes of the slice: x: 2, y: 2, z: 4, core: 2. Of those that a mesh axis runs over, the one named last changes fastest.
Arguments:
- frames: bfloat16 [128, 128, 1024], P(('dp', 'fsdp')), may hold values from -6 to 6
- frame_mask: int32 [128, 128], P(('dp', 'fsdp')), may hold values 0 or 1
- motion_weight: bfloat16 [1024, 512], replicated, may hold values from -0.1875 to 0.1875
- caption_feats: bfloat16 [2048, 4096], P(('dp', 'fsdp')), may hold values from -6 to 6
- text_weight: bfloat16 [4096, 512], P('fsdp'), may hold values from -0.09375 to 0.09375
- caption_route: int32 [2048, 1], P(('dp', 'fsdp')), may hold values from 0 to 7; in each aligned block of 64 rows (0 to 63, 64 to 127, ...) at most 16 rows name the same one
- caption_clip: int32 [2048], P(('dp', 'fsdp')), may hold values from 0 to 15
Outputs:
- clip_loss: float32 [128], P(('dp', 'fsdp'))
- motion_grad: float32 [128, 512], P(('dp', 'fsdp'))
Inputs may be any that keep to these rules, and one draw needn't show every extreme that they name: `caption_route`: no group is named by more than 16 of one device's captions; in some devices' captions one group is named exactly 16 times.
All inputs are finite; a program needn't handle non-finite values. No bound on the sum of `frame_mask` on one device may be relied on, other than what follows from the above.
Results may differ from a plain program's by a relative error of at most 0.0037.
Values may be sent and summed in bfloat16 or wider, within the bound.
A program may use at most 64 MiB of HBM per device.

v0:
```python
import jax
import jax.numpy as jnp
from jax import lax
from jax.sharding import PartitionSpec as P


def normalize(values):
    return (values * lax.rsqrt(jnp.sum(values * values, axis=-1, keepdims=True) + 1e-06)).astype(
        jnp.bfloat16
    )


def local(
    frames, frame_mask, motion_weight, caption_feats, text_weight, caption_route, caption_clip
):
    clip_dev, frame_count, feat_width = frames.shape
    cap_dev = caption_feats.shape[0]
    emb_width = motion_weight.shape[1]
    groups = lax.axis_size("dp")
    slot_count = max(2, 2 * cap_dev // groups)
    text_raw = jnp.dot(
        caption_feats,
        lax.all_gather(text_weight, "fsdp", axis=0, tiled=True),
        preferred_element_type=jnp.float32,
    )
    text_emb = normalize(text_raw)
    hidden = jax.nn.gelu(
        jnp.dot(frames.reshape(-1, feat_width), motion_weight, preferred_element_type=jnp.float32)
    )
    hidden = hidden.reshape(clip_dev, frame_count, emb_width)
    pooled = jnp.sum(hidden * frame_mask.astype(jnp.float32)[:, :, None], axis=1)
    motion_emb = normalize(pooled)
    target = caption_route[:, 0]
    order = jnp.arange(cap_dev, dtype=jnp.int32)
    earlier = (target[:, None] == target[None, :]) & (order[None, :] < order[:, None])
    ranking = jnp.sum(earlier.astype(jnp.int32), axis=1)
    position = target * slot_count + ranking
    placing = position[:, None] == jnp.arange(groups * slot_count, dtype=jnp.int32)[None, :]
    send_text = jnp.einsum(
        "rs,re->se", placing.astype(jnp.bfloat16), text_emb, preferred_element_type=jnp.float32
    ).astype(jnp.bfloat16)
    send_clip = jnp.sum(jnp.where(placing, caption_clip[:, None] + 1, 0), axis=0) - 1
    recv_text, recv_clip = (
        lax.all_to_all(
            send_text.reshape(groups, slot_count, emb_width),
            "dp",
            split_axis=0,
            concat_axis=0,
            tiled=True,
        ),
        lax.all_to_all(
            send_clip.reshape(groups, slot_count), "dp", split_axis=0, concat_axis=0, tiled=True
        ),
    )
    group_motion = lax.all_gather(motion_emb, "fsdp", axis=0, tiled=True)
    grp_clips = group_motion.shape[0]
    arrived = recv_text.reshape(-1, emb_width)
    arrived_clip = recv_clip.reshape(-1)
    scores = (
        jnp.einsum("se,me->sm", arrived, group_motion, preferred_element_type=jnp.float32) / 0.07
    )
    lse_vals = jnp.log(jnp.sum(jnp.exp(scores), axis=1))
    onehot = (arrived_clip[:, None] == jnp.arange(grp_clips, dtype=jnp.int32)[None, :]).astype(
        jnp.float32
    )
    losses = lse_vals - jnp.sum(onehot * scores, axis=1)
    present = (arrived_clip >= 0)[:, None]
    coefficient = jnp.where(present, jnp.exp(scores - lse_vals[:, None]) - onehot, 0.0).astype(
        jnp.bfloat16
    )
    grad_term = jnp.einsum("sm,se->me", coefficient, arrived, preferred_element_type=jnp.float32)
    loss_term = jnp.sum(onehot * losses[:, None], axis=0)
    grad_sum, loss_sum = (
        lax.psum_scatter(grad_term, "fsdp", scatter_dimension=0, tiled=True),
        lax.psum_scatter(loss_term, "fsdp", scatter_dimension=0, tiled=True),
    )
    clip_loss = loss_sum * (clip_dev / cap_dev)
    motion_grad = grad_sum / 0.07
    return (clip_loss, motion_grad)


def solution(mesh):
    in_specs = (
        P(("dp", "fsdp"), None, None),
        P(("dp", "fsdp"), None),
        P(),
        P(("dp", "fsdp"), None),
        P("fsdp", None),
        P(("dp", "fsdp"), None),
        P(("dp", "fsdp")),
    )
    out_specs = (P(("dp", "fsdp")), P(("dp", "fsdp"), None))
    return jax.shard_map(local, mesh=mesh, in_specs=in_specs, out_specs=out_specs, check_vma=False)
```

profile of v0, /device:TPU:0, one launch (start us, length us, event | category | flops | bytes accessed | tf_op | source)
XLA Modules:
  0.0 83.7 jit_solution(15372083720051974493)
XLA Ops:
  7.2 0.0 copy-start
  7.2 0.0 copy-start.1
  7.2 0.0 all-gather.3.cloned.1.call-start
  7.2 0.7 all-gather.3.cloned.1.call-update
  7.9 0.9 %convert_reduce_fusion = s32[64]{0:T(128)S(1)} fusion(s32[64]{0:T(128)} %bitcast.26), kind=kLoop, calls=%fused_computation.16 | loop fusion | flops 20416 | bytes 512 | tf_op jit(solution)/shard_map/reduce_sum | solution.py:36
  8.8 0.7 broadcast_add_fusion.1
  9.5 0.7 fusion.16
  10.2 0.1 select_reduce_fusion
  10.3 0.7 sub.25
  10.9 7.3 %all-to-all-start = ((s32[8,1,16]{2,1,0:T(1,128)}), s32[8,1,16]{2,1,0:T(1,128)S(1)}, u32[]{:S(2)}, u32[]{:S(2)}) async-start(s32[8,1,16]{2,1,0:T(1,128)} %bitcast.3), calls=%async_computation | async-start | bytes 8192 | tf_op jit(solution)/shard_map/all_to_all | solution.py:51
  18.2 0.7 convert_element_type.25
  18.9 2.3 %multiply_reduce_fusion = f32[4,512]{1,0:T(4,128)S(1)} fusion(f32[4,128]{1,0:T(4,128)S(1)} %convert_element_type.25, bf16[512,1024]{1,0:T(8,128)(2,1)S(1)} %bitcast.23, bf16[1024,512]{1,0:T(8,128)(2,1)} %param.9), kind=kOutput, calls=%fused_computation.10 | convolution fusion | flops 539490304 | bytes 2107392 | tf_op jit(solution)/shard_map/dot_general | solution.py:28
  21.2 0.1 multiply_reduce_fusion.2
  21.3 0.1 fusion.10
  21.4 25.4 %all-gather.3.cloned.1.call-done = bf16[4096,512]{1,0:T(8,128)(2,1)} async-done(((bf16[1024,512]{1,0:T(8,128)(2,1)}), bf16[4096,512]{1,0:T(8,128)(2,1)}) %all-gather.3.cloned.1.call-update) | async-done | bytes 4194320 | tf_op jit(solution)/shard_map/all_gather | solution.py:23
  46.8 3.3 %multiply_reduce_fusion.1 = (f32[64]{0:T(128)S(1)}, f32[64,512]{1,0:T(8,128)S(1)}) fusion(bf16[64,4096]{1,0:T(8,128)(2,1)} %param.10, bf16[4096,512]{1,0:T(8,128)(2,1)} %all-gather.3.cloned.1.call-done), kind=kOutput, calls=%fused_computation.12 | convolution fusion | flops 268500928 | bytes 4849920 | tf_op jit(solution)/shard_map/dot_general | solution.py:21
  50.2 0.9 %convolution_convert_fusion = bf16[128,512]{1,0:T(8,128)(2,1)} fusion(f32[64,512]{1,0:T(8,128)S(1)} %get-tuple-element.9, f32[64]{0:T(128)S(1)} %add_rsqrt_fusion.1, s32[64]{0:T(128)S(1)} %fusion.16), kind=kOutput, calls=%fused_computation.1 | convolution fusion | flops 8527872 | bytes 262656 | tf_op jit(solution)/shard_map/rs,re->se/dot_general | solution.py:39
  51.1 0.0 all-to-all-done
  51.1 5.5 %all-to-all-start.1 = ((bf16[8,16,512]{2,1,0:T(8,128)(2,1)}), bf16[8,16,512]{2,1,0:T(8,128)(2,1)S(1)}, u32[]{:S(2)}, u32[]{:S(2)}) async-start(bf16[8,16,512]{2,1,0:T(8,128)(2,1)} %bitcast.4), calls=%async_computation.1 | async-start | bytes 262144 | tf_op jit(solution)/shard_map/all_to_all | solution.py:44
  56.6 5.2 %all-gather = bf16[4,4,512]{2,1,0:T(4,128)(2,1)S(1)} all-gather(bf16[1,4,512]{2,1,0:T(4,128)(2,1)S(1)} %fusion.10), channel_id=1, replica_groups=mesh['dp'=8,'fsdp'=4] {'fsdp'}, dimensions={0}, use_global_device_ids=true | all-gather | bytes 20480 | tf_op jit(solution)/shard_map/all_gather | solution.py:55
  61.8 0.0 copy-done.1
  61.8 0.6 dynamic-slice
  63.0 0.5 broadcast.60
  63.6 0.7 reduce.3
  64.2 0.1 eq.53
  64.3 0.0 all-to-all-done.1
  64.3 0.2 exponential_reduce_fusion
  64.5 0.1 select_reduce_fusion.1
  64.6 0.1 fusion.11
  64.8 10.9 %all-reduce.2 = (f32[16]{0:T(128)S(1)}, f32[16,512]{1,0:T(8,128)S(1)}) all-reduce(f32[16]{0:T(128)S(1)} %select_reduce_fusion.1, f32[16,512]{1,0:T(8,128)S(1)} %fusion.11), channel_id=2, replica_groups=mesh['dp'=8,'fsdp'=4] {'fsdp'}, use_global_device_ids=true, to_apply=%region_8.9.clone | all-reduce | flops 8208 | bytes 65664
  75.7 0.6 dynamic-slice_multiply_fusion
  76.3 0.6 dynamic-slice_multiply_fusion.1
  (7 shorter events, 0.0 us)
Async XLA Ops:
  7.2 11.7 %copy-start = (bf16[4,128,1024]{2,1,0:T(8,128)(2,1)S(1)}, bf16[4,128,1024]{2,1,0:T(8,128)(2,1)}, u32[]{:S(2)}) copy-start(bf16[4,128,1024]{2,1,0:T(8,128)(2,1)} %param.7) | copy-start | bytes 3145732
  7.2 54.6 %copy-start.1 = (u32[32]{0:T(128)S(1)}, u32[32]{0:T(128)}, u32[]{:S(2)}) copy-start(u32[32]{0:T(128)} %constant.36) | copy-start | bytes 388
  7.2 39.7 %all-gather.3.cloned.1.call-start = ((), (), s32[]{:S(2)}) async-start(), calls=%async_computation.2 | async-start | bytes 5242880 | tf_op jit(solution)/shard_map/all_gather | solution.py:23
  10.9 40.2 %all-to-all-start = ((s32[8,1,16]{2,1,0:T(1,128)}), s32[8,1,16]{2,1,0:T(1,128)S(1)}, u32[]{:S(2)}, u32[]{:S(2)}) async-start(s32[8,1,16]{2,1,0:T(1,128)} %bitcast.3), calls=%async_computation | async-start | bytes 8192 | tf_op jit(solution)/shard_map/all_to_all | solution.py:51
  51.1 13.2 %all-to-all-start.1 = ((bf16[8,16,512]{2,1,0:T(8,128)(2,1)}), bf16[8,16,512]{2,1,0:T(8,128)(2,1)S(1)}, u32[]{:S(2)}, u32[]{:S(2)}) async-start(bf16[8,16,512]{2,1,0:T(8,128)(2,1)} %bitcast.4), calls=%async_computation.1 | async-start | bytes 262144 | tf_op jit(solution)/shard_map/all_to_all | solution.py:44
Sparse Core Ops, SparseCore 0:
  9.6 37.2 all-gather.2
where the time goes:
time: 84.1 us; the launch traced here: 83.7 us
  waiting for transfers between devices  26.1 us (31%)
  blocking collectives  16.1 us (19%)
  between operations  14.8 us (18%)
  starting transfers between devices  12.8 us (15%)
  matrix products  6.87 us (8%)
  other arithmetic  5.21 us (6%)
  local copies, waits for them, and re-layouts  1.88 us (2%)
    all_gather x1, waiting for transfers between devices, local(): lax.all_gather(text_weight, 'fsdp', axis=0, tiled=True)  25.4 us
    unnamed x1, blocking collectives  10.9 us
    all_to_all x1, starting transfers between devices, local(): lax.all_to_all(send_clip.reshape(groups, slot_count), 'dp', split_axis=0,...  7.25 us
    all_to_all x1, starting transfers between devices, local(): lax.all_to_all(send_text.reshape(groups, slot_count, emb_width), 'dp', sp...  5.51 us
    all_gather x1, blocking collectives, local(): group_motion = lax.all_gather(motion_emb, 'fsdp', axis=0, tiled=True)  5.17 us
    dot_general x1, matrix products, local(): jnp.dot(caption_feats, lax.all_gather(text_weight, 'fsdp', axis=0, tiled=...  3.3 us
    dot_general x1, matrix products, local(): jnp.dot(frames.reshape(-1, feat_width), motion_weight, preferred_element_...  2.32 us
  transfers between devices with their start and end apart: 3, of which 1 were waited for; matrix products, arithmetic and copies ran while one was open for 15% of the time, Pallas kernels for 0%

commit v1 on v0

v1 whole, which is shorter than its diff:
```python
import functools

import jax
import jax.numpy as jnp
from jax import lax
from jax.experimental import pallas as pl
from jax.experimental.pallas import tpu as pltpu
from jax.sharding import PartitionSpec as P

HALVES = 2
LOSS_LANES = 128
F32 = jnp.float32
BF16 = jnp.bfloat16


def normalize(values):
    return values * lax.rsqrt(jnp.sum(values * values, axis=-1, keepdims=True) + 1e-06)


def gelu(x):
    return 0.5 * x * (1.0 + jnp.tanh(0.7978845608028654 * (x + 0.044715 * (x * x * x))))


def remote(src, dst, send, recv, axis, index):
    return pltpu.make_async_remote_copy(
        src_ref=src,
        dst_ref=dst,
        send_sem=send,
        recv_sem=recv,
        device_id={axis: index},
        device_id_type=pl.DeviceIdType.MESH,
    )


def kernel(
    groups,
    shards,
    frames_hbm,
    weight_hbm,
    caps_hbm,
    text_hbm,
    mask_ref,
    route_ref,
    clip_ref,
    grad_out,
    loss_out,
    frames_v,
    weight_v,
    own_caps,
    text_v,
    cap_recv,
    part_send,
    part_recv,
    clip_slots,
    grp_rows,
    all_motion,
    grad_send,
    grad_recv,
    sum_slots,
    sum_recv,
    local_sem,
    cap_ss,
    cap_rs,
    part_ss,
    part_rs,
    m1_ss,
    m1_rs,
    m2_ss,
    m2_rs,
    g1_ss,
    g1_rs,
    g2_ss,
    g2_rs,
):
    me_g, me_f = lax.axis_index("dp"), lax.axis_index("fsdp")
    clip_dev, frame_count, _ = frames_v.shape
    cap_dev, depth = own_caps.shape
    emb = text_v.shape[1]
    rows = cap_dev // HALVES
    block = groups * clip_dev
    clips = block * shards

    def shard(k):
        return lax.rem(me_f + (k + shards), shards)

    def group(k):
        return lax.rem(me_g + (k + groups), groups)

    def columns(owner):
        return pl.ds(pl.multiple_of(owner * depth, depth), depth)

    loads = [
        pltpu.make_async_copy(frames_hbm, frames_v, local_sem.at[0]),
        pltpu.make_async_copy(weight_hbm, weight_v, local_sem.at[1]),
        pltpu.make_async_copy(text_hbm, text_v, local_sem.at[2]),
        pltpu.make_async_copy(caps_hbm.at[:, columns(me_f)], own_caps, local_sem.at[3]),
    ]
    for load in loads:
        load.start()

    barrier = pltpu.get_barrier_semaphore()
    for k in range(1, shards):
        pl.semaphore_signal(
            barrier, inc=1, device_id={"fsdp": shard(k)}, device_id_type=pl.DeviceIdType.MESH
        )
    for k in range(1, groups):
        pl.semaphore_signal(
            barrier, inc=1, device_id={"dp": group(k)}, device_id_type=pl.DeviceIdType.MESH
        )
    pl.semaphore_wait(barrier, shards + groups - 2)

    offsets = sorted(range(1, shards), key=lambda k: abs(k - shards // 2))
    cap_copies = {}
    for h in range(HALVES):
        for k in offsets:
            cap_copies[h, k] = remote(
                caps_hbm.at[pl.ds(h * rows, rows), columns(shard(k))],
                cap_recv.at[h, k - 1],
                cap_ss.at[h, k - 1],
                cap_rs.at[h, k - 1],
                "fsdp",
                shard(k),
            )
            cap_copies[h, k].start()

    loads[0].wait()
    loads[1].wait()
    eye = (
        lax.broadcasted_iota(jnp.int32, (frame_count, frame_count), 0)
        == lax.broadcasted_iota(jnp.int32, (frame_count, frame_count), 1)
    ).astype(F32)
    for clip in range(clip_dev):
        hidden = gelu(jnp.dot(frames_v[clip], weight_v[...], preferred_element_type=F32))
        keep = jnp.sum(eye * mask_ref[pl.ds(clip, 1), :].astype(F32), axis=1, keepdims=True)
        pooled = jnp.sum(hidden * keep, axis=0, keepdims=True)
        clip_slots[me_f, pl.ds(clip, 1), :] = normalize(pooled).astype(BF16).astype(F32)
    m1 = []
    for k in range(1, shards):
        copy = remote(
            clip_slots.at[me_f],
            clip_slots.at[me_f],
            m1_ss.at[k - 1],
            m1_rs.at[k - 1],
            "fsdp",
            shard(k),
        )
        copy.start()
        m1.append(copy)

    loads[2].wait()
    loads[3].wait()
    text_raw = jnp.dot(own_caps[...], text_v[...], preferred_element_type=F32)
    part_copies = []

    def project(h):
        for k in offsets:
            cap_copies[h, k].wait_recv()
        arrived = cap_recv[h].reshape((shards - 1) * rows, depth)
        partial = jnp.dot(arrived, text_v[...], preferred_element_type=F32).astype(BF16)
        for k in offsets:
            part_send[h, k - 1] = partial[(k - 1) * rows : k * rows, :]
            copy = remote(
                part_send.at[h, k - 1],
                part_recv.at[k - 1, pl.ds(h * rows, rows)],
                part_ss.at[h, k - 1],
                part_rs.at[h, k - 1],
                "fsdp",
                shard(-k),
            )
            copy.start()
            part_copies.append(copy)

    project(0)

    for k in range(1, shards):
        remote(
            clip_slots.at[me_f],
            clip_slots.at[shard(-k)],
            m1_ss.at[k - 1],
            m1_rs.at[k - 1],
            "fsdp",
            shard(-k),
        ).wait_recv()
    for f in range(shards):
        grp_rows[pl.ds(f * clip_dev, clip_dev), :] = clip_slots[f]
    all_motion[me_g] = grp_rows[...].astype(BF16)
    m2 = []
    for k in range(1, groups):
        copy = remote(
            all_motion.at[me_g],
            all_motion.at[me_g],
            m2_ss.at[k - 1],
            m2_rs.at[k - 1],
            "dp",
            group(k),
        )
        copy.start()
        m2.append(copy)

    for h in range(1, HALVES):
        project(h)

    for k in range(1, groups):
        remote(
            all_motion.at[me_g],
            all_motion.at[group(-k)],
            m2_ss.at[k - 1],
            m2_rs.at[k - 1],
            "dp",
            group(-k),
        ).wait_recv()
    gathered = all_motion[...].reshape(clips, emb)
    pieces = []
    for f in range(shards):
        r = lax.broadcasted_iota(jnp.int32, (block, clips), 0)
        c = lax.broadcasted_iota(jnp.int32, (block, clips), 1)
        want = (r // clip_dev) * (clip_dev * shards) + f * clip_dev + (r & (clip_dev - 1))
        pick = (c == want).astype(F32).astype(BF16)
        pieces.append(jnp.dot(pick, gathered, preferred_element_type=F32).astype(BF16))
    motion = jnp.concatenate(pieces, axis=0)

    route, chosen = route_ref[...], clip_ref[...]
    r = lax.broadcasted_iota(jnp.int32, (clips, cap_dev), 0)
    in_group = ((r & (block - 1)) // clip_dev) == route
    target = in_group & (((r // block) * clip_dev + (r & (clip_dev - 1))) == chosen)

    for copy in part_copies:
        copy.wait_recv()
    for k in range(1, shards):
        text_raw = text_raw + part_recv[k - 1].astype(F32)
    text_emb = normalize(text_raw).astype(BF16)

    scores = (
        lax.dot_general(motion, text_emb, (((1,), (1,)), ((), ())), preferred_element_type=F32)
        / 0.07
    )
    power = jnp.where(in_group, jnp.exp(scores), 0.0)
    total = jnp.sum(power, axis=0, keepdims=True)
    lse = jnp.log(total)
    onehot = target.astype(F32)
    losses = lse - jnp.sum(onehot * scores, axis=0, keepdims=True)
    coefficient = (power * (1.0 / total) - onehot).astype(BF16)
    grad = jnp.dot(coefficient, text_emb, preferred_element_type=F32)
    loss_term = jnp.sum(onehot * losses, axis=1, keepdims=True)
    high = loss_term.astype(BF16).astype(F32)
    lane = lax.broadcasted_iota(jnp.int32, (clips, LOSS_LANES), 1)
    loss_pair = jnp.where(lane < LOSS_LANES // 2, high, loss_term - high).astype(BF16)
    grad = grad.astype(BF16)
    g1 = []
    for f in range(shards):
        grad_send[f, :, pl.ds(0, emb)] = grad[f * block : (f + 1) * block, :]
        grad_send[f, :, pl.ds(emb, LOSS_LANES)] = loss_pair[f * block : (f + 1) * block, :]
    for k in offsets:
        copy = remote(
            grad_send.at[shard(k)],
            grad_recv.at[k - 1],
            g1_ss.at[k - 1],
            g1_rs.at[k - 1],
            "fsdp",
            shard(k),
        )
        copy.start()
        g1.append(copy)
    summed = grad_send[me_f].astype(F32)
    for copy in g1:
        copy.wait_recv()
    for k in range(1, shards):
        summed = summed + grad_recv[k - 1].astype(F32)
    for g in range(groups):
        sum_slots[g] = summed[g * clip_dev : (g + 1) * clip_dev, :]
    g2 = []
    for k in range(1, groups):
        copy = remote(
            sum_slots.at[group(k)],
            sum_recv.at[k - 1],
            g2_ss.at[k - 1],
            g2_rs.at[k - 1],
            "dp",
            group(k),
        )
        copy.start()
        g2.append(copy)
    final = sum_slots[me_g]
    for copy in g2:
        copy.wait_recv()
    for k in range(1, groups):
        final = final + sum_recv[k - 1]
    grad_out[...] = final[:, :emb] / 0.07
    loss = final[:, emb : emb + 1] + final[:, emb + LOSS_LANES // 2 : emb + LOSS_LANES // 2 + 1]
    corner = lax.broadcasted_iota(
        jnp.int32, (clip_dev, clip_dev), 0
    ) == lax.broadcasted_iota(jnp.int32, (clip_dev, clip_dev), 1)
    loss_out[...] = jnp.sum(jnp.where(corner, loss, 0.0), axis=0, keepdims=True) * (
        clip_dev / cap_dev
    )

    for copy in [*cap_copies.values(), *part_copies, *m1, *m2, *g1, *g2]:
        copy.wait_send()


def local(
    frames, frame_mask, motion_weight, caption_feats, text_weight, caption_route, caption_clip
):
    groups, shards = lax.axis_size("dp"), lax.axis_size("fsdp")
    clip_dev = frames.shape[0]
    cap_dev = caption_feats.shape[0]
    depth, emb = text_weight.shape
    rows = cap_dev // HALVES
    block = groups * clip_dev
    wide = emb + LOSS_LANES
    hbm, vmem = pl.BlockSpec(memory_space=pl.ANY), pl.BlockSpec(memory_space=pltpu.VMEM)
    dma = pltpu.SemaphoreType.DMA
    grad, loss = pl.pallas_call(
        functools.partial(kernel, groups, shards),
        out_shape=(
            jax.ShapeDtypeStruct((clip_dev, emb), F32),
            jax.ShapeDtypeStruct((1, clip_dev), F32),
        ),
        in_specs=[hbm] * 4 + [vmem] * 3,
        out_specs=(vmem, vmem),
        scratch_shapes=[
            pltpu.VMEM(frames.shape, BF16),
            pltpu.VMEM(motion_weight.shape, BF16),
            pltpu.VMEM((cap_dev, depth), BF16),
            pltpu.VMEM((depth, emb), BF16),
            pltpu.VMEM((HALVES, shards - 1, rows, depth), BF16),
            pltpu.VMEM((HALVES, shards - 1, rows, emb), BF16),
            pltpu.VMEM((shards - 1, cap_dev, emb), BF16),
            pltpu.VMEM((shards, clip_dev, emb), F32),
            pltpu.VMEM((shards * clip_dev, emb), F32),
            pltpu.VMEM((groups, shards * clip_dev, emb), BF16),
            pltpu.VMEM((shards, block, wide), BF16),
            pltpu.VMEM((shards - 1, block, wide), BF16),
            pltpu.VMEM((groups, clip_dev, wide), F32),
            pltpu.VMEM((groups - 1, clip_dev, wide), F32),
            dma((4,)),
            dma((HALVES, shards - 1)),
            dma((HALVES, shards - 1)),
            dma((HALVES, shards - 1)),
            dma((HALVES, shards - 1)),
            dma((shards - 1,)),
            dma((shards - 1,)),
            dma((groups - 1,)),
            dma((groups - 1,)),
            dma((shards - 1,)),
            dma((shards - 1,)),
            dma((groups - 1,)),
            dma((groups - 1,)),
        ],
        compiler_params=pltpu.CompilerParams(
            collective_id=0, has_side_effects=True, vmem_limit_bytes=56 * 1024 * 1024
        ),
    )(
        frames,
        motion_weight,
        caption_feats,
        text_weight,
        frame_mask,
        caption_route.reshape(1, cap_dev),
        caption_clip.reshape(1, cap_dev),
    )
    return loss.reshape(clip_dev), grad


def solution(mesh):
    in_specs = (
        P(("dp", "fsdp"), None, None),
        P(("dp", "fsdp"), None),
        P(),
        P(("dp", "fsdp"), None),
        P("fsdp", None),
        P(("dp", "fsdp"), None),
        P(("dp", "fsdp")),
    )
    out_specs = (P(("dp", "fsdp")), P(("dp", "fsdp"), None))
    return jax.shard_map(local, mesh=mesh, in_specs=in_specs, out_specs=out_specs, check_vma=False)
```

time: 84.1 us -> 32.4 us (0.39)
  Pallas kernels: 0 us -> 29.1 us
  waiting for transfers between devices: 26.1 us -> 0 us
  blocking collectives: 16.1 us -> 0 us
  between operations: 14.8 us -> 0.65 us
  starting transfers between devices: 12.8 us -> 0 us
  matrix products: 6.87 us -> 0 us
  other arithmetic: 5.21 us -> 0 us
    pallas_call x0 -> x1, Pallas kernels: none -> 29.1 us  [local(): pl.pallas_call(functools.partial(kernel, groups, shards), out_shape=(jax....]
    all_gather x1 -> x0, waiting for transfers between devices: 25.4 us -> none  [local(): lax.all_gather(text_weight, 'fsdp', axis=0, tiled=True)]
    all_to_all x2 -> x0, starting transfers between devices: 12.8 us -> none  [the longest x1 7.25 us: local(): lax.all_to_all(send_clip.reshape(groups, slot_count), 'dp', split_axis=0,...]
    unnamed x1 -> x0, blocking collectives: 10.9 us -> none
    dot_general x5 -> x0, matrix products: 6.87 us -> none  [the longest x1 3.3 us: local(): jnp.dot(caption_feats, lax.all_gather(text_weight, 'fsdp', axis=0, tiled=...]
    all_gather x1 -> x0, blocking collectives: 5.17 us -> none  [local(): group_motion = lax.all_gather(motion_emb, 'fsdp', axis=0, tiled=True)]
    unnamed x6 -> x4, local copies, waits for them, and re-layouts: 0.61 us -> 2.47 us
    reduce_sum x4 -> x0, other arithmetic: 1.24 us -> none  [the longest x1 0.91 us: local(): ranking = jnp.sum(earlier.astype(jnp.int32), axis=1)]
  transfers between devices with their start and end apart: 3 -> 0, of which waited for: 1 -> 0; matrix products, arithmetic and copies ran while one was open for 15% -> 0% of each run, Pallas kernels for 0% -> 0%
where the time goes in v1:
time: 32.4 us; the launch traced here: 32.2 us
  Pallas kernels  29.1 us (90%)
  local copies, waits for them, and re-layouts  2.47 us (8%)
  between operations  0.65 us (2%)
    pallas_call x1, Pallas kernels, local(): pl.pallas_call(functools.partial(kernel, groups, shards), out_shape=(jax....  29.1 us
    unnamed x4, local copies, waits for them, and re-layouts  2.47 us

profile of v1, /device:TPU:0, one launch (start us, length us, event | category | flops | bytes accessed | tf_op | source)
XLA Modules:
  0.0 32.2 jit_solution(16539153008765895661)
XLA Ops:
  0.6 29.1 %shard_map.86 = (f32[4,512]{1,0:T(4,128)}, f32[1,4]{1,0:T(1,128)}) custom-call(bf16[4,128,1024]{2,1,0:T(8,128)(2,1)} %frames_hbm.1, bf16[1024,512]{1,0:T(8,128)(2,1)} %weight_hbm.1, bf16[64,4096]{1,0:T(8,128)(2,1)} %caps_hbm.1, bf16[1024,512]{1,0:T(8,128)(2,1)} %text_hbm.1, s32[4,128]{1,0:T(4,128)} %mask_ref.1, s32[1,64]{1,0:T(1,128)} %bitcast.3, ...), custom_call_target="tpu_custom_call" | custom-call | tf_op jit(solution)/shard_map/pallas_call | solution.py:313
  29.7 0.0 copy-start
  29.8 0.7 %copy-done = f32[1,4]{1,0:T(1,128)S(1)} copy-done((f32[1,4]{1,0:T(1,128)S(1)}, f32[1,4]{1,0:T(1,128)}, u32[]{:S(2)}) %copy-start) | copy-done | bytes 40
  30.4 0.5 %copy.11 = f32[4]{0:T(128)} copy(f32[4]{0:T(128)S(1)} %bitcast.5) | data formatting | bytes 32
  30.9 1.3 %copy.12 = f32[4,512]{1,0:T(4,128)} copy(f32[4,512]{1,0:T(4,128)} %get-tuple-element.9) | data formatting | bytes 16384
Async XLA Ops:
  29.7 0.7 %copy-start = (f32[1,4]{1,0:T(1,128)S(1)}, f32[1,4]{1,0:T(1,128)}, u32[]{:S(2)}) copy-start(f32[1,4]{1,0:T(1,128)} %get-tuple-element.4) | copy-start | bytes 52

commit v2 on v1

v2 whole, which is shorter than its diff:
```python
import functools

import jax
import jax.numpy as jnp
from jax import lax
from jax.experimental import pallas as pl
from jax.experimental.pallas import tpu as pltpu
from jax.sharding import PartitionSpec as P

HALVES = 2
LANES = 128
F32 = jnp.float32
BF16 = jnp.bfloat16


def normalize(values):
    return values * lax.rsqrt(jnp.sum(values * values, axis=-1, keepdims=True) + 1e-06)


def gelu(x):
    return 0.5 * x * (1.0 + jnp.tanh(0.7978845608028654 * (x + 0.044715 * (x * x * x))))


def remote(src, dst, send, recv, target):
    return pltpu.make_async_remote_copy(
        src_ref=src,
        dst_ref=dst,
        send_sem=send,
        recv_sem=recv,
        device_id=target,
        device_id_type=pl.DeviceIdType.MESH,
    )


def kernel(
    groups,
    shards,
    frames_hbm,
    weight_hbm,
    caps_hbm,
    text_hbm,
    mask_ref,
    route_ref,
    clip_ref,
    grad_out,
    loss_out,
    frames_v,
    weight_v,
    own_caps,
    text_v,
    cap_recv,
    part_send,
    part_recv,
    clip_slots,
    grp_rows,
    all_motion,
    grad_send,
    grad_recv,
    loss_send,
    loss_recv,
    local_sem,
    cap_ss,
    cap_rs,
    part_ss,
    part_rs,
    m1_ss,
    m1_rs,
    m2_ss,
    m2_rs,
    g_ss,
    g_rs,
):
    me_g, me_f = lax.axis_index("dp"), lax.axis_index("fsdp")
    clip_dev, frame_count, _ = frames_v.shape
    cap_dev, depth = own_caps.shape
    emb = text_v.shape[1]
    rows = cap_dev // HALVES
    grp_clips = shards * clip_dev
    clips = groups * grp_clips
    devices = groups * shards
    me = me_g * shards + me_f

    def shard(k):
        return lax.rem(me_f + (k + shards), shards)

    def group(k):
        return lax.rem(me_g + (k + groups), groups)

    def columns(owner):
        return pl.ds(pl.multiple_of(owner * depth, depth), depth)

    loads = [
        pltpu.make_async_copy(frames_hbm, frames_v, local_sem.at[0]),
        pltpu.make_async_copy(weight_hbm, weight_v, local_sem.at[1]),
        pltpu.make_async_copy(text_hbm, text_v, local_sem.at[2]),
        pltpu.make_async_copy(caps_hbm.at[:, columns(me_f)], own_caps, local_sem.at[3]),
    ]
    for load in loads:
        load.start()

    barrier = pltpu.get_barrier_semaphore()
    for k in range(1, shards):
        pl.semaphore_signal(
            barrier, inc=1, device_id={"fsdp": shard(k)}, device_id_type=pl.DeviceIdType.MESH
        )
    for k in range(1, groups):
        pl.semaphore_signal(
            barrier, inc=1, device_id={"dp": group(k)}, device_id_type=pl.DeviceIdType.MESH
        )
    pl.semaphore_wait(barrier, shards + groups - 2)

    offsets = sorted(range(1, shards), key=lambda k: abs(k - shards // 2))
    cap_copies = {}

    def send_captions(h):
        for k in offsets:
            cap_copies[h, k] = remote(
                caps_hbm.at[pl.ds(h * rows, rows), columns(shard(k))],
                cap_recv.at[h, k - 1],
                cap_ss.at[h, k - 1],
                cap_rs.at[h, k - 1],
                {"fsdp": shard(k)},
            )
            cap_copies[h, k].start()

    send_captions(0)

    loads[0].wait()
    loads[1].wait()
    eye = (
        lax.broadcasted_iota(jnp.int32, (frame_count, frame_count), 0)
        == lax.broadcasted_iota(jnp.int32, (frame_count, frame_count), 1)
    ).astype(F32)
    for clip in range(clip_dev):
        hidden = gelu(jnp.dot(frames_v[clip], weight_v[...], preferred_element_type=F32))
        keep = jnp.sum(eye * mask_ref[pl.ds(clip, 1), :].astype(F32), axis=1, keepdims=True)
        pooled = jnp.sum(hidden * keep, axis=0, keepdims=True)
        clip_slots[me_f, pl.ds(clip, 1), :] = normalize(pooled).astype(BF16).astype(F32)
    m1 = []
    for k in range(1, shards):
        copy = remote(
            clip_slots.at[me_f],
            clip_slots.at[me_f],
            m1_ss.at[k - 1],
            m1_rs.at[k - 1],
            {"fsdp": shard(k)},
        )
        copy.start()
        m1.append(copy)

    for h in range(1, HALVES):
        send_captions(h)

    loads[2].wait()
    loads[3].wait()
    text_raw = jnp.dot(own_caps[...], text_v[...], preferred_element_type=F32)
    part_copies = []

    for k in range(1, shards):
        remote(
            clip_slots.at[me_f],
            clip_slots.at[shard(-k)],
            m1_ss.at[k - 1],
            m1_rs.at[k - 1],
            {"fsdp": shard(-k)},
        ).wait_recv()
    for f in range(shards):
        grp_rows[pl.ds(f * clip_dev, clip_dev), :] = clip_slots[f]
    all_motion[me_g] = grp_rows[...].astype(BF16)
    m2 = []
    for k in range(1, groups):
        copy = remote(
            all_motion.at[me_g],
            all_motion.at[me_g],
            m2_ss.at[k - 1],
            m2_rs.at[k - 1],
            {"dp": group(k)},
        )
        copy.start()
        m2.append(copy)

    def project(h):
        for k in offsets:
            cap_copies[h, k].wait_recv()
        arrived = cap_recv[h].reshape((shards - 1) * rows, depth)
        partial = jnp.dot(arrived, text_v[...], preferred_element_type=F32).astype(BF16)
        for k in offsets:
            part_send[h, k - 1] = partial[(k - 1) * rows : k * rows, :]
            copy = remote(
                part_send.at[h, k - 1],
                part_recv.at[k - 1, pl.ds(h * rows, rows)],
                part_ss.at[h, k - 1],
                part_rs.at[h, k - 1],
                {"fsdp": shard(-k)},
            )
            copy.start()
            part_copies.append(copy)

    for h in range(HALVES):
        project(h)

    for k in range(1, groups):
        remote(
            all_motion.at[me_g],
            all_motion.at[group(-k)],
            m2_ss.at[k - 1],
            m2_rs.at[k - 1],
            {"dp": group(-k)},
        ).wait_recv()
    motion = all_motion[...].reshape(clips, emb)

    route, chosen = route_ref[...], clip_ref[...]
    r = lax.broadcasted_iota(jnp.int32, (clips, cap_dev), 0)
    in_group = (r // grp_clips) == route
    target = r == route * grp_clips + chosen

    for copy in part_copies:
        copy.wait_recv()
    for k in range(1, shards):
        text_raw = text_raw + part_recv[k - 1].astype(F32)
    text_emb = normalize(text_raw).astype(BF16)

    scores = (
        lax.dot_general(motion, text_emb, (((1,), (1,)), ((), ())), preferred_element_type=F32)
        / 0.07
    )
    power = jnp.where(in_group, jnp.exp(scores), 0.0)
    total = jnp.sum(power, axis=0, keepdims=True)
    lse = jnp.log(total)
    onehot = target.astype(F32)
    losses = lse - jnp.sum(onehot * scores, axis=0, keepdims=True)
    coefficient = (power * (1.0 / total) - onehot).astype(BF16)
    grad = jnp.dot(coefficient, text_emb, preferred_element_type=F32)
    loss_term = jnp.sum(onehot * losses, axis=1, keepdims=True)
    lane = lax.broadcasted_iota(jnp.int32, (clips, LANES), 1)
    row = lax.broadcasted_iota(jnp.int32, (clips, LANES), 0)
    spread = jnp.where(lane == (row & (clip_dev - 1)), loss_term, 0.0)
    owner = (
        lax.broadcasted_iota(jnp.int32, (devices, clips), 1) // clip_dev
        == lax.broadcasted_iota(jnp.int32, (devices, clips), 0)
    )
    owner = owner.astype(F32).astype(BF16)
    high = spread.astype(BF16)
    low = (spread - high.astype(F32)).astype(BF16)
    loss_rows = jnp.dot(owner, high, preferred_element_type=F32) + jnp.dot(
        owner, low, preferred_element_type=F32
    )
    loss_send[...] = loss_rows.reshape(devices, 1, LANES)
    grad = grad.reshape(devices // 2, 2 * clip_dev, emb)
    upper = lax.broadcasted_iota(jnp.int32, (devices // 2, 2 * clip_dev, LANES), 1) < clip_dev
    even, odd = [], []
    for c in range(0, emb // LANES, 2):
        one = grad[:, :, c * LANES : (c + 1) * LANES]
        two = grad[:, :, (c + 1) * LANES : (c + 2) * LANES]
        even.append(jnp.where(upper, one, pltpu.roll(two, clip_dev, axis=1)))
        odd.append(jnp.where(upper, pltpu.roll(one, clip_dev, axis=1), two))
    grad_send[:, 0] = jnp.concatenate(even, axis=1).astype(BF16)
    grad_send[:, 1] = jnp.concatenate(odd, axis=1).astype(BF16)

    def to_owner(step, carry):
        k = step
        to = lax.rem(me + k, devices)
        where = {"dp": to // shards, "fsdp": lax.rem(to, shards)}
        remote(
            grad_send.at[to // 2, lax.rem(to, 2)], grad_recv.at[k - 1], g_ss.at[0], g_rs.at[0], where
        ).start()
        remote(loss_send.at[to], loss_recv.at[k - 1], g_ss.at[1], g_rs.at[1], where).start()
        return carry

    lax.fori_loop(1, devices, to_owner, 0)
    where = {"dp": me_g, "fsdp": shard(1)}
    grad_all = remote(grad_recv, grad_recv, g_ss.at[0], g_rs.at[0], where)
    loss_all = remote(loss_recv, loss_recv, g_ss.at[1], g_rs.at[1], where)
    grad_all.wait_recv()
    final = grad_send[me // 2, lax.rem(me, 2)].astype(F32)
    final = (final + jnp.sum(grad_recv[...].astype(F32), axis=0)) / 0.07
    for c in range(emb // LANES):
        grad_out[:, pl.ds(c * LANES, LANES)] = final[c * clip_dev : (c + 1) * clip_dev, :]
    loss_all.wait_recv()
    loss = loss_send[me] + jnp.sum(loss_recv[...], axis=0)
    loss_out[...] = loss * (clip_dev / cap_dev)

    grad_all.wait_send()
    loss_all.wait_send()
    for copy in [*cap_copies.values(), *part_copies, *m1, *m2]:
        copy.wait_send()


def local(
    frames, frame_mask, motion_weight, caption_feats, text_weight, caption_route, caption_clip
):
    groups, shards = lax.axis_size("dp"), lax.axis_size("fsdp")
    clip_dev = frames.shape[0]
    cap_dev = caption_feats.shape[0]
    depth, emb = text_weight.shape
    rows = cap_dev // HALVES
    devices = groups * shards
    sub = clip_dev * emb // LANES
    limit = (56 if devices <= 64 else 56) * 1024 * 1024
    hbm, vmem = pl.BlockSpec(memory_space=pltpu.HBM), pl.BlockSpec(memory_space=pltpu.VMEM)
    dma = pltpu.SemaphoreType.DMA
    grad, loss = pl.pallas_call(
        functools.partial(kernel, groups, shards),
        out_shape=(
            jax.ShapeDtypeStruct((clip_dev, emb), F32),
            jax.ShapeDtypeStruct((1, LANES), F32),
        ),
        in_specs=[hbm] * 4 + [vmem] * 3,
        out_specs=(vmem, vmem),
        scratch_shapes=[
            pltpu.VMEM(frames.shape, BF16),
            pltpu.VMEM(motion_weight.shape, BF16),
            pltpu.VMEM((cap_dev, depth), BF16),
            pltpu.VMEM((depth, emb), BF16),
            pltpu.VMEM((HALVES, shards - 1, rows, depth), BF16),
            pltpu.VMEM((HALVES, shards - 1, rows, emb), BF16),
            pltpu.VMEM((shards - 1, cap_dev, emb), BF16),
            pltpu.VMEM((shards, clip_dev, emb), F32),
            pltpu.VMEM((shards * clip_dev, emb), F32),
            pltpu.VMEM((groups, shards * clip_dev, emb), BF16),
            pltpu.VMEM((devices // 2, 2, sub, LANES), BF16),
            pltpu.VMEM((devices - 1, sub, LANES), BF16),
            pltpu.VMEM((devices, 1, LANES), F32),
            pltpu.VMEM((devices - 1, 1, LANES), F32),
            dma((4,)),
            dma((HALVES, shards - 1)),
            dma((HALVES, shards - 1)),
            dma((HALVES, shards - 1)),
            dma((HALVES, shards - 1)),
            dma((shards - 1,)),
            dma((shards - 1,)),
            dma((groups - 1,)),
            dma((groups - 1,)),
            dma((2,)),
            dma((2,)),
        ],
        compiler_params=pltpu.CompilerParams(
            collective_id=0, has_side_effects=True, vmem_limit_bytes=limit
        ),
    )(
        frames,
        motion_weight,
        caption_feats,
        text_weight,
        frame_mask,
        caption_route.reshape(1, cap_dev),
        caption_clip.reshape(1, cap_dev),
    )
    return loss[0, :clip_dev], grad


def solution(mesh):
    in_specs = (
        P(("dp", "fsdp"), None, None),
        P(("dp", "fsdp"), None),
        P(),
        P(("dp", "fsdp"), None),
        P("fsdp", None),
        P(("dp", "fsdp"), None),
        P(("dp", "fsdp")),
    )
    out_specs = (P(("dp", "fsdp")), P(("dp", "fsdp"), None))
    return jax.shard_map(local, mesh=mesh, in_specs=in_specs, out_specs=out_specs, check_vma=False)
```

time: 32.4 us -> 28 us (0.86)
  Pallas kernels: 29.1 us -> 24.7 us
    pallas_call x1, Pallas kernels: 29.1 us -> 24.7 us  [local(): pl.pallas_call(functools.partial(kernel, groups, shards), out_shape=(jax....]
    squeeze x0 -> x1, local copies, waits for them, and re-layouts: none -> 0.51 us  [local(): return (loss[0, :clip_dev], grad)]
    unnamed x4 -> x3, local copies, waits for them, and re-layouts: 2.47 us -> 1.95 us
where the time goes in v2:
time: 28 us; the launch traced here: 27.8 us
  Pallas kernels  24.7 us (88%)
  local copies, waits for them, and re-layouts  2.47 us (9%)
  between operations  0.65 us (2%)
    pallas_call x1, Pallas kernels, local(): pl.pallas_call(functools.partial(kernel, groups, shards), out_shape=(jax....  24.7 us
    unnamed x3, local copies, waits for them, and re-layouts  1.95 us

profile of v2, /device:TPU:0, one launch (start us, length us, event | category | flops | bytes accessed | tf_op | source)
XLA Modules:
  0.0 27.8 jit_solution(7964361711691035179)
XLA Ops:
  0.6 24.7 %shard_map.86 = (f32[4,512]{1,0:T(4,128)}, f32[1,128]{1,0:T(1,128)}) custom-call(bf16[4,128,1024]{2,1,0:T(8,128)(2,1)} %frames_hbm.1, bf16[1024,512]{1,0:T(8,128)(2,1)} %weight_hbm.1, bf16[64,4096]{1,0:T(8,128)(2,1)} %caps_hbm.1, bf16[1024,512]{1,0:T(8,128)(2,1)} %text_hbm.1, s32[4,128]{1,0:T(4,128)} %mask_ref.1, s32[1,64]{1,0:T(1,128)} %bitcast.4, ...), custom_call_target="tpu_custom_call" | custom-call | tf_op jit(solution)/shard_map/pallas_call | solution.py:302
  25.3 0.0 copy-start
  25.3 0.7 %copy-done = f32[1,128]{1,0:T(1,128)S(1)} copy-done((f32[1,128]{1,0:T(1,128)S(1)}, f32[1,128]{1,0:T(1,128)}, u32[]{:S(2)}) %copy-start) | copy-done | bytes 536
  26.0 0.5 %slice_bitcast_fusion = f32[4]{0:T(128)} fusion(f32[1,128]{1,0:T(1,128)S(1)} %copy-done), kind=kLoop, calls=%fused_computation | loop fusion | bytes 32 | tf_op jit(solution)/shard_map/squeeze | solution.py:349
  26.5 1.3 %copy.10 = f32[4,512]{1,0:T(4,128)} copy(f32[4,512]{1,0:T(4,128)} %get-tuple-element.9) | data formatting | bytes 16384
Async XLA Ops:
  25.3 0.7 %copy-start = (f32[1,128]{1,0:T(1,128)S(1)}, f32[1,128]{1,0:T(1,128)}, u32[]{:S(2)}) copy-start(f32[1,128]{1,0:T(1,128)} %get-tuple-element.4) | copy-start | bytes 1540
